TPU v7x, 512 devices: a whole 4x8x8 slice. The times are simulated.
512 devices in a mesh: col: 16 (over x, z_hi, core), row: 32 (over y, z_lo).
Axes of the slice: x: 4, y: 8, z: 8 (z_hi: 2, z_lo: 4; z = z_hi * 4 + z_lo), core: 2. Of those that a mesh axis runs over, the one named last changes fastest.
Arguments:
- features: bfloat16 [131072, 256], P(('col', 'row')), may hold values from -6 to 6
- tiles: bfloat16 [32768, 128, 128], P(('col', 'row')), as said below
- tile_dst: int32 [32768], P(('col', 'row')), may hold values from 0 to 63
- tile_src: int32 [32768], P(('col', 'row')), may hold values from 0 to 1
- weight: bfloat16 [256, 256], replicated, may hold values from -0.375 to 0.375
- bias: float32 [256], replicated, may hold values from -3 to 3
Outputs:
- activated: bfloat16 [131072, 256], P(('col', 'row'))
Inputs may be any that keep to these rules, and one draw needn't show every extreme that they name: `tiles`: entries are zero or positive edge weights; about one in 32 entries of a tile is nonzero.
All inputs are finite; a program needn't handle non-finite values.
Results may differ from a plain program's by a relative error of at most 0.022.
Values may be sent and summed in bfloat16 or wider, within the bound.
No kernel may reach another device: no remote copies, remote signals or barrier semaphores. Data moves between devices by JAX's collectives and lax.ppermute only.
A program may use at most 64 MiB of HBM per device.

v0:
```python
import math

import jax
import jax.numpy as jnp
from jax import lax
from jax.sharding import PartitionSpec as P


def from_behind(block, axis, distance):
    devices = range(lax.axis_size(axis))
    route = [((i - distance) % len(devices), i) for i in devices]
    return lax.ppermute(block, axis, route)


def shards(features, tiles, tile_dst, tile_src, weight, bias):
    tile_count = tiles.shape[0]
    tile_size = tiles.shape[1]
    width = features.shape[1]
    src_blocks = features.reshape(features.shape[0] // tile_size, tile_size, width)
    local_blocks = src_blocks.shape[0]
    col_count = lax.axis_size("col")
    window_count = 2 * col_count * local_blocks
    labels = jnp.arange(window_count, dtype=jnp.int32)
    group_size = math.gcd(tile_count, 32)
    group_total = tile_count // group_size

    def add_group(index, total):
        offset = index * group_size
        tile_group = lax.dynamic_slice_in_dim(tiles, offset, group_size, 0)
        src_group = lax.dynamic_slice_in_dim(tile_src, offset, group_size, 0)
        dst_group = lax.dynamic_slice_in_dim(tile_dst, offset, group_size, 0)
        picked = src_blocks[src_group]
        prods = jnp.einsum("tij,tjh->tih", tile_group, picked, preferred_element_type=jnp.float32)
        select = (dst_group[None, :] == labels[:, None]).astype(jnp.float32)
        return total + jnp.einsum("bt,tih->bih", select, prods, preferred_element_type=jnp.float32)

    start_total = jnp.zeros((window_count, tile_size, width), jnp.float32)
    summed = lax.fori_loop(0, group_total, add_group, start_total)
    partial_value = summed.astype(jnp.bfloat16)
    partial_rows = partial_value.reshape(window_count * tile_size, width)
    owned = lax.psum_scatter(
        partial_rows.astype(jnp.float32).astype(jnp.bfloat16),
        "col",
        scatter_dimension=0,
        tiled=True,
    ).astype(jnp.float32)
    owned = owned.reshape(2, local_blocks * tile_size, width)
    passed = from_behind(owned[1].astype(jnp.bfloat16), "row", 1).astype(jnp.float32)
    aggregate = owned[0] + passed
    aggregate_b = aggregate.astype(jnp.bfloat16)
    mixed = jnp.dot(aggregate_b, weight, preferred_element_type=jnp.float32) + bias
    return jnp.maximum(mixed, 0.0).astype(jnp.bfloat16)


def solution(mesh):
    in_specs = (
        P(("col", "row"), None),
        P(("col", "row"), None, None),
        P(("col", "row")),
        P(("col", "row")),
        P(),
        P(),
    )
    out_specs = P(("col", "row"), None)
    return jax.shard_map(shards, mesh=mesh, in_specs=in_specs, out_specs=out_specs, check_vma=False)
```

profile of v0, /device:TPU:1, one launch (start us, length us, event | category | flops | bytes accessed | tf_op | source)
XLA Modules:
  0.0 178.2 jit_solution(12131204212375161961)
XLA Ops:
  6.5 0.0 copy-start
  6.5 0.0 reduce-scatter.2.cloned.1.call-start
  6.5 25.1 %while.14 = (s32[]{:T(128)}, f32[64,128,256]{2,0,1:T(8,128)}, s32[64]{0:T(128)}, bf16[64,128,128]{2,1,0:T(8,128)(2,1)}, s32[64]{0:T(128)}, /*index=5*/bf16[2,128...) while((s32[]{:T(128)}, f32[64,128,256]{2,0,1:T(8,128)}, s32[64]{0:T(128)}, ...), condition=%wide.region_1.0_spmd.clone, body=%wide.region_0.0_spmd.clone.sunk | while | flops 406850656 | bytes 28316720 | solution.py:38
  6.5 0.8 compare_select_fusion.2
  7.3 0.7 dynamic_slice.32
  8.0 1.6 gather_fusion
  9.6 1.9 %fusion.26 = bf16[32,128,256]{2,1,0:T(8,128)(2,1)S(1)} fusion(bf16[32,128,256]{2,1,0:T(8,128)(2,1)S(1)} %gather_fusion, bf16[64,128,128]{2,1,0:T(8,128)(2,1)} %get-tuple-element.225, s32[]{:T(128)S(6)} %select_n.22), kind=kOutput, calls=%fused_computation.5.clone.1 | convolution fusion | flops 268435456 | bytes 5242884 | tf_op jit(solution)/shard_map/while/body/eval_jaxpr/tij,tjh->tih/dot_general | solution.py:33
  11.6 5.9 %select_add_fusion.2 = f32[64,128,256]{2,0,1:T(8,128)} fusion(f32[64,128,256]{2,0,1:T(8,128)} %get-tuple-element.213, pred[]{:T(512)S(6)} %compare.3, bf16[32,128,256]{2,1,0:T(8,128)(2,1)S(1)} %fusion.26, s32[32]{0:T(128)S(1)} %dynamic_slice.32), kind=kOutput, calls=%fused_computation.2.clone.1 | convolution fusion | flops 138414080 | bytes 18874496 | tf_op jit(solution)/shard_map/while/body/eval_jaxpr/bt,tih->bih/dot_general | solution.py:35
  17.4 0.7 compare_select_fusion.2
  18.1 0.7 dynamic_slice.32
  18.9 1.6 gather_fusion
  20.5 1.9 %fusion.26 = bf16[32,128,256]{2,1,0:T(8,128)(2,1)S(1)} fusion(bf16[32,128,256]{2,1,0:T(8,128)(2,1)S(1)} %gather_fusion, bf16[64,128,128]{2,1,0:T(8,128)(2,1)} %get-tuple-element.225, s32[]{:T(128)S(6)} %select_n.22), kind=kOutput, calls=%fused_computation.5.clone.1 | convolution fusion | flops 268435456 | bytes 5242884 | tf_op jit(solution)/shard_map/while/body/eval_jaxpr/tij,tjh->tih/dot_general | solution.py:33
  22.4 9.2 %select_add_fusion.2 = f32[64,128,256]{2,0,1:T(8,128)} fusion(f32[64,128,256]{2,0,1:T(8,128)} %get-tuple-element.213, pred[]{:T(512)S(6)} %compare.3, bf16[32,128,256]{2,1,0:T(8,128)(2,1)S(1)} %fusion.26, s32[32]{0:T(128)S(1)} %dynamic_slice.32), kind=kOutput, calls=%fused_computation.2.clone.1 | convolution fusion | flops 138414080 | bytes 18874496 | tf_op jit(solution)/shard_map/while/body/eval_jaxpr/bt,tih->bih/dot_general | solution.py:35
  31.6 9.8 %copy.14 = bf16[64,128,256]{2,1,0:T(8,128)(2,1)} copy(f32[64,128,256]{2,0,1:T(8,128)} %get-tuple-element.129) | data formatting | bytes 12582912 | tf_op jit(solution)/shard_map/while | solution.py:38
  41.4 0.0 copy-start.1
  41.4 0.0 reduce-scatter.2.cloned.1.call-update
  41.4 117.6 %reduce-scatter.2.cloned.1.call-done = bf16[512,256]{1,0:T(8,128)(2,1)} async-done(((bf16[8192,256]{1,0:T(8,128)(2,1)}), bf16[512,256]{1,0:T(8,128)(2,1)}) %reduce-scatter.2.cloned.1.call-update) | async-done | bytes 262160 | tf_op jit(solution)/shard_map/reduce_scatter | solution.py:41
  159.0 0.9 slice.18
  160.0 2.2 %collective-permute-start = (bf16[256,256]{1,0:T(8,128)(2,1)S(1)}, bf16[256,256]{1,0:T(8,128)(2,1)S(1)}, u32[]{:S(2)}, u32[]{:S(2)}) collective-permute-start(bf16[256,256]{1,0:T(8,128)(2,1)S(1)} %slice.18), channel_id=1, source_target_pairs={{31,0},{0,1},{1,2},{2,3},{3,4},{4,5},{5,6},{6,7},{7,8},{8,9},{9,10... | collective-permute-start | bytes 393224 | tf_op jit(solution)/shard_map/ppermute | solution.py:12
  162.2 7.4 %collective-permute-done = bf16[256,256]{1,0:T(8,128)(2,1)S(1)} collective-permute-done((bf16[256,256]{1,0:T(8,128)(2,1)S(1)}, bf16[256,256]{1,0:T(8,128)(2,1)S(1)}, u32[]{:S(2)}, u32[]{:S(2)}) %collective-permute-start) | collective-permute-done | bytes 131104 | tf_op jit(solution)/shard_map/ppermute | solution.py:12
  169.6 0.0 copy-done
  169.6 0.0 copy-done.1
  169.6 1.8 fusion.13
  (3 shorter events, 0.0 us)
Async XLA Ops:
  6.5 163.0 %copy-start = (bf16[256,256]{1,0:T(8,128)(2,1)S(1)}, bf16[256,256]{1,0:T(8,128)(2,1)}, u32[]{:S(2)}) copy-start(bf16[256,256]{1,0:T(8,128)(2,1)} %param.12) | copy-start | bytes 393220
  6.5 152.5 %reduce-scatter.2.cloned.1.call-start = ((), (), s32[]{:S(2)}) async-start(), calls=%async_computation.1 | async-start | bytes 4456448 | tf_op jit(solution)/shard_map/reduce_scatter | solution.py:41
  41.4 128.2 %copy-start.1 = (f32[256]{0:T(256)S(1)}, f32[256]{0:T(256)}, u32[]{:S(2)}) copy-start(f32[256]{0:T(256)} %param.13) | copy-start | bytes 3076
  160.0 9.6 %collective-permute-start = (bf16[256,256]{1,0:T(8,128)(2,1)S(1)}, bf16[256,256]{1,0:T(8,128)(2,1)S(1)}, u32[]{:S(2)}, u32[]{:S(2)}) collective-permute-start(bf16[256,256]{1,0:T(8,128)(2,1)S(1)} %slice.18), channel_id=1, source_target_pairs={{31,0},{0,1},{1,2},{2,3},{3,4},{4,5},{5,6},{6,7},{7,8},{8,9},{9,10... | collective-permute-start | bytes 393224 | tf_op jit(solution)/shard_map/ppermute | solution.py:12
Sparse Core Ops, SparseCore 0:
  41.5 117.4 reduce-scatter.1
where the time goes:
time: 180 us; the launch traced here: 178 us
  waiting for transfers between devices  125 us (69%)
  matrix products  20.7 us (12%)
  local copies, waits for them, and re-layouts  15.3 us (8%)
  between operations  13.4 us (7%)
  starting transfers between devices  2.25 us (1%)
    reduce_scatter x1, waiting for transfers between devices, shards(): lax.psum_scatter(partial_rows.astype(jnp.float32).astype(jnp.bfloat16), '...  118 us
    dot_general x2, matrix products, add_group(): jnp.einsum('bt,tih->bih', select, prods, preferred_element_type=jnp.float32)  15.1 us
    while x1, local copies, waits for them, and re-layouts, shards(): summed = lax.fori_loop(0, group_total, add_group, start_total)  9.77 us
    ppermute x1, waiting for transfers between devices, from_behind(): return lax.ppermute(block, axis, route)  7.36 us
    dot_general x2, matrix products, add_group(): jnp.einsum('tij,tjh->tih', tile_group, picked, preferred_element_type=jnp...  3.84 us
  transfers between devices with their start and end apart: 2, of which 2 were waited for; matrix products, arithmetic and copies ran while one was open for 0% of the time, Pallas kernels for 0%

commit v1 on v0

v1 whole, which is shorter than its diff:
```python
import jax
import jax.numpy as jnp
from jax import lax
from jax.experimental import pallas as pl
from jax.experimental.pallas import tpu as pltpu
from jax.sharding import PartitionSpec as P

N_X, N_HI, N_CORE, N_ROW = 4, 2, 2, 32
AXES = ("col", "row")
GROUP = 8


def route(move):
    pairs = []
    for c in range(N_X * N_HI * N_CORE):
        for r in range(N_ROW):
            x, hi, core, row = move(c // 4, (c // 2) % 2, c % 2, r)
            target = ((x % N_X) * 4 + hi * 2 + core) * N_ROW + row % N_ROW
            pairs.append((c * N_ROW + r, target))
    return pairs


def send(block, move):
    return lax.ppermute(block, AXES, route(move))


def chip_sums(meta, dst_a, src_a, dst_b, src_b, tiles_a, tiles_b, feats_a, feats_b):
    count, size, _ = tiles_a.shape
    width = feats_a.shape[-1]

    def kernel(meta, dst_a, src_a, dst_b, src_b, tiles_a, tiles_b, feats_a, feats_b, *rest):
        outs, acc, todo = rest[:N_X], rest[N_X], rest[N_X + 1]
        x_here, wanted = meta[0], meta[1]
        acc[...] = jnp.zeros_like(acc)

        def run(dst, src, tiles, feats):
            def scan(i, n):
                slot = dst[i]
                place = (((slot >> 4) - x_here) & 3) * 4 + (slot & 3)
                todo[n] = i | (src[i] << 8) | (place << 16)
                return n + (((slot >> 2) & 3) == wanted).astype(jnp.int32)

            n = lax.fori_loop(0, count, scan, 0, unroll=8)
            for j in range(GROUP - 1):
                todo[n + j] = 16 << 16

            def add(g, carry):
                items = [todo[g * GROUP + j] for j in range(GROUP)]
                prods = [
                    jnp.dot(tiles[e & 255], feats[(e >> 8) & 255], preferred_element_type=jnp.float32)
                    for e in items
                ]
                for e, prod in zip(items, prods):
                    acc[e >> 16] += prod
                return carry

            lax.fori_loop(0, (n + GROUP - 1) // GROUP, add, 0)

        run(dst_a, src_a, tiles_a, feats_a)
        run(dst_b, src_b, tiles_b, feats_b)
        for d, out in enumerate(outs):
            out[...] = acc[4 * d : 4 * d + 4].reshape(4 * size, width).astype(out.dtype)

    smem = pl.BlockSpec(memory_space=pltpu.SMEM)
    vmem = pl.BlockSpec(memory_space=pltpu.VMEM)
    return pl.pallas_call(
        kernel,
        out_shape=[jax.ShapeDtypeStruct((4 * size, width), jnp.bfloat16)] * N_X,
        in_specs=[smem] * 5 + [vmem] * 4,
        out_specs=[vmem] * N_X,
        scratch_shapes=[pltpu.VMEM((17, size, width), jnp.float32), pltpu.SMEM((count + GROUP,), jnp.int32)],
        compiler_params=pltpu.CompilerParams(vmem_limit_bytes=32 * 2**20),
        cost_estimate=pl.CostEstimate(flops=32 * 2 * size * size * width, bytes_accessed=7 * 2**20, transcendentals=0),
    )(meta, dst_a, src_a, dst_b, src_b, tiles_a, tiles_b, feats_a, feats_b)


def over_x(parts):
    far = send(parts[2], lambda x, hi, core, row: (x + 2, hi, core, row))
    right = send(parts[1], lambda x, hi, core, row: (x + 1, hi, core, row))
    left = send(parts[3], lambda x, hi, core, row: (x - 1, hi, core, row))
    return [parts[0], right, left, far]


def total(parts):
    result = parts[0].astype(jnp.float32)
    for part in parts[1:]:
        result = result + part.astype(jnp.float32)
    return result


def shards(features, tiles, tile_dst, tile_src, weight, bias):
    count, size, _ = tiles.shape
    width = features.shape[1]
    blocks = features.shape[0] // size
    col = lax.axis_index("col")
    x_here, hi_here, core_here = col // 4, (col // 2) % 2, col % 2

    def other_core(block):
        return send(block, lambda x, hi, core, row: (x, hi, 1 - core, row))

    their_tiles = other_core(tiles)
    slots = jnp.zeros((16, width), jnp.bfloat16)
    slots = slots.at[0, :count].set(tile_dst.astype(jnp.bfloat16)).at[1, :count].set(tile_src.astype(jnp.bfloat16))
    theirs = other_core(jnp.concatenate([features, slots], axis=0))
    their_feats = theirs[: blocks * size]
    their_dst = theirs[blocks * size, :count].astype(jnp.int32)
    their_src = theirs[blocks * size + 1, :count].astype(jnp.int32)

    def sums_for(hi):
        meta = jnp.stack([x_here, hi * 2 + core_here]).astype(jnp.int32)
        return chip_sums(
            meta, tile_dst, tile_src, their_dst, their_src, tiles, their_tiles,
            features.reshape(blocks, size, width), their_feats.reshape(blocks, size, width),
        )

    half = blocks * size
    away = over_x(sums_for(1 - hi_here))
    home = over_x(sums_for(hi_here))
    away_sum = total(away).astype(jnp.bfloat16)
    same_row = send(away_sum[:half], lambda x, hi, core, row: (x, 1 - hi, core, row))
    next_row = send(away_sum[half:], lambda x, hi, core, row: (x, 1 - hi, core, row + 1))
    passed = total([part[half:] for part in home]).astype(jnp.bfloat16)
    passed = send(passed, lambda x, hi, core, row: (x, hi, core, row + 1))
    aggregate = total([part[:half] for part in home] + [same_row, next_row, passed])
    mixed = jnp.dot(aggregate.astype(jnp.bfloat16), weight, preferred_element_type=jnp.float32) + bias
    return jnp.maximum(mixed, 0.0).astype(jnp.bfloat16)


def solution(mesh):
    in_specs = (
        P(("col", "row"), None),
        P(("col", "row"), None, None),
        P(("col", "row")),
        P(("col", "row")),
        P(),
        P(),
    )
    out_specs = P(("col", "row"), None)
    return jax.shard_map(shards, mesh=mesh, in_specs=in_specs, out_specs=out_specs, check_vma=False)
```

time: 180 us -> 66.1 us (0.37)
  waiting for transfers between devices: 125 us -> 11.9 us
  starting transfers between devices: 2.25 us -> 40.1 us
  matrix products: 20.7 us -> 0.92 us
  between operations: 13.4 us -> 0.29 us
  local copies, waits for them, and re-layouts: 15.3 us -> 3.94 us
  Pallas kernels: 0 us -> 5.92 us
    reduce_scatter x1 -> x0, waiting for transfers between devices: 118 us -> none  [shards(): lax.psum_scatter(partial_rows.astype(jnp.float32).astype(jnp.bfloat16), '...]
    ppermute x1 -> x11, starting transfers between devices: 2.25 us -> 40.1 us  [send(): return lax.ppermute(block, AXES, route(move))]
    dot_general x5 -> x1, matrix products: 20.7 us -> 0.92 us  [shards(): jnp.dot(aggregate.astype(jnp.bfloat16), weight, preferred_element_type=jn...]
    while x1 -> x0, local copies, waits for them, and re-layouts: 9.77 us -> none  [shards(): summed = lax.fori_loop(0, group_total, add_group, start_total)]
    pallas_call x0 -> x2, Pallas kernels: none -> 5.92 us  [chip_sums(): pl.pallas_call(kernel, out_shape=[jax.ShapeDtypeStruct((4 * size, width),...]
    ppermute x1 -> x11, waiting for transfers between devices: 7.36 us -> 11.9 us  [send(): return lax.ppermute(block, AXES, route(move))]
    unnamed x4 -> x16, local copies, waits for them, and re-layouts: 0.01 us -> 3.82 us
    gather x2 -> x0, local copies, waits for them, and re-layouts: 3.17 us -> none  [add_group(): picked = src_blocks[src_group]]
  transfers between devices with their start and end apart: 2 -> 11, of which waited for: 2 -> 2; matrix products, arithmetic and copies ran while one was open for 0% -> 4% of each run, Pallas kernels for 0% -> 4%
where the time goes in v1:
time: 66.1 us; the launch traced here: 65.6 us
  starting transfers between devices  40.1 us (61%)
  waiting for transfers between devices  11.9 us (18%)
  Pallas kernels  5.92 us (9%)
  local copies, waits for them, and re-layouts  3.94 us (6%)
  other arithmetic  2.53 us (4%)
  matrix products  0.92 us (1%)
    ppermute x11, starting transfers between devices, send(): return lax.ppermute(block, AXES, route(move))  40.1 us
    ppermute x11, waiting for transfers between devices, send(): return lax.ppermute(block, AXES, route(move))  11.9 us
    pallas_call x2, Pallas kernels, chip_sums(): pl.pallas_call(kernel, out_shape=[jax.ShapeDtypeStruct((4 * size, width),...  5.92 us
    unnamed x16, local copies, waits for them, and re-layouts  3.82 us
  transfers between devices with their start and end apart: 11, of which 2 were waited for; matrix products, arithmetic and copies ran while one was open for 4% of the time, Pallas kernels for 4%

profile of v1, /device:TPU:1, one launch (start us, length us, event | category | flops | bytes accessed | tf_op | source)
XLA Modules:
  0.0 65.6 jit_solution(6353334786125189642)
XLA Ops:
  0.0 8.9 %collective-permute-start.1 = (bf16[64,128,128]{2,1,0:T(8,128)(2,1)}, bf16[64,128,128]{2,1,0:T(8,128)(2,1)S(1)}, u32[]{:S(2)}, u32[]{:S(2)}) collective-permute-start(bf16[64,128,128]{2,1,0:T(8,128)(2,1)} %tiles_a.3), channel_id=1, source_target_pairs={{0,32},{1,33},{2,34},{3,35},{4,36},{5,37},{6,38},{7,39},{8,40},{9,... | collective-permute-start | bytes 6291464 | tf_op jit(solution)/shard_map/ppermute | solution.py:24
  8.9 0.7 %convert_bitcast_fusion.1 = bf16[1,64]{1,0:T(2,128)(2,1)S(1)} fusion(s32[64]{0:T(128)} %dst_a.3), kind=kLoop, calls=%fused_computation.18 | loop fusion | flops 64 | bytes 384 | tf_op jit(solution)/shard_map/reshape.58
  9.6 0.7 %convert_bitcast_fusion = bf16[1,64]{1,0:T(2,128)(2,1)S(1)} fusion(s32[64]{0:T(128)} %src_a.3), kind=kLoop, calls=%fused_computation.17 | loop fusion | flops 64 | bytes 384 | tf_op jit(solution)/shard_map/reshape.41
  10.2 0.1 scatter.9
  10.3 0.9 %pad_maximum_fusion = bf16[272,256]{1,0:T(8,128)(2,1)S(1)} fusion(bf16[16,256]{1,0:T(8,128)(2,1)S(1)} %scatter.9, bf16[256,256]{1,0:T(8,128)(2,1)} %param.10), kind=kLoop, calls=%fused_computation.6 | loop fusion | flops 278528 | bytes 278528 | tf_op jit(solution)/shard_map/concatenate | solution.py:104
  11.3 1.9 %collective-permute-start = (bf16[272,256]{1,0:T(8,128)(2,1)S(1)}, bf16[272,256]{1,0:T(8,128)(2,1)S(1)}, u32[]{:S(2)}, u32[]{:S(2)}) collective-permute-start(bf16[272,256]{1,0:T(8,128)(2,1)S(1)} %pad_maximum_fusion), channel_id=1, source_target_pairs={{0,32},{1,33},{2,34},{3,35},{4,36},{5,37},{6,38},{7,39},{8,40},{9,... | collective-permute-start | bytes 417800 | tf_op jit(solution)/shard_map/ppermute | solution.py:24
  13.2 0.1 pad_add_fusion
  13.3 1.2 %collective-permute-done = bf16[272,256]{1,0:T(8,128)(2,1)S(1)} collective-permute-done((bf16[272,256]{1,0:T(8,128)(2,1)S(1)}, bf16[272,256]{1,0:T(8,128)(2,1)S(1)}, u32[]{:S(2)}, u32[]{:S(2)}) %collective-permute-start) | collective-permute-done | bytes 139296 | tf_op jit(solution)/shard_map/ppermute | solution.py:24
  14.6 0.0 copy-start.1
  14.6 1.6 %copy-done.1 = bf16[64,128,128]{2,1,0:T(8,128)(2,1)S(1)} copy-done((bf16[64,128,128]{2,1,0:T(8,128)(2,1)S(1)}, bf16[64,128,128]{2,1,0:T(8,128)(2,1)}, u32[]{:S(2)}) %copy-start.1) | copy-done | bytes 2097176
  16.1 0.9 %copy-done.3 = bf16[256,256]{1,0:T(8,128)(2,1)S(1)} copy-done((bf16[256,256]{1,0:T(8,128)(2,1)S(1)}, bf16[256,256]{1,0:T(8,128)(2,1)}, u32[]{:S(2)}) %copy-start.3) | copy-done | bytes 131096
  17.1 0.7 copy-done.4
  17.7 0.7 copy-done.6
  18.4 3.1 %shard_map.65 = (bf16[512,256]{1,0:T(8,128)(2,1)S(1)}, bf16[512,256]{1,0:T(8,128)(2,1)S(1)}, bf16[512,256]{1,0:T(8,128)(2,1)S(1)}, bf16[512,256]{1,0:T(8,128)(2,1)S(1)}) custom-call(s32[2]{0:T(128)S(1)} %get-tuple-element.50.meta, s32[64]{0:T(128)S(1)} %copy-done.4, s32[64]{0:T(128)S(1)} %copy-done.6, s32[64]{0:T(128)S(1)} %get-tuple-element.48.dst_b, ...), custom_call_target="tpu_custom_call" | custom-call | flops 268435456 | bytes 7340032 | tf_op jit(solution)/shard_map/pallas_call | solution.py:66
  21.5 1.9 %collective-permute-start.5 = (bf16[512,256]{1,0:T(8,128)(2,1)S(1)}, bf16[512,256]{1,0:T(8,128)(2,1)S(1)}, u32[]{:S(2)}, u32[]{:S(2)}) collective-permute-start(bf16[512,256]{1,0:T(8,128)(2,1)S(1)} %get-tuple-element.42), channel_id=1, source_target_pairs={{0,128},{1,129},{2,130},{3,131},{4,132},{5,133},{6,134},{7,135},{8... | collective-permute-start | bytes 786440 | tf_op jit(solution)/shard_map/ppermute | solution.py:24
  23.4 4.6 %collective-permute-start.6 = (bf16[512,256]{1,0:T(8,128)(2,1)S(1)}, bf16[512,256]{1,0:T(8,128)(2,1)S(1)}, u32[]{:S(2)}, u32[]{:S(2)}) collective-permute-start(bf16[512,256]{1,0:T(8,128)(2,1)S(1)} %get-tuple-element.43), channel_id=1, source_target_pairs={{0,384},{1,385},{2,386},{3,387},{4,388},{5,389},{6,390},{7,391},{8... | collective-permute-start | bytes 786440 | tf_op jit(solution)/shard_map/ppermute | solution.py:24
  28.0 1.9 %collective-permute-start.7 = (bf16[512,256]{1,0:T(8,128)(2,1)S(1)}, bf16[512,256]{1,0:T(8,128)(2,1)S(1)}, u32[]{:S(2)}, u32[]{:S(2)}) collective-permute-start(bf16[512,256]{1,0:T(8,128)(2,1)S(1)} %get-tuple-element.44), channel_id=1, source_target_pairs={{0,256},{1,257},{2,258},{3,259},{4,260},{5,261},{6,262},{7,263},{8... | collective-permute-start | bytes 786440 | tf_op jit(solution)/shard_map/ppermute | solution.py:24
  29.9 2.8 %shard_map.64 = (bf16[512,256]{1,0:T(8,128)(2,1)S(1)}, bf16[512,256]{1,0:T(8,128)(2,1)S(1)}, bf16[512,256]{1,0:T(8,128)(2,1)S(1)}, bf16[512,256]{1,0:T(8,128)(2,1)S(1)}) custom-call(s32[2]{0:T(128)S(1)} %get-tuple-element.49.meta, s32[64]{0:T(128)S(1)} %copy-done.5, s32[64]{0:T(128)S(1)} %copy-done.6, s32[64]{0:T(128)S(1)} %get-tuple-element.48.dst_b, ...), custom_call_target="tpu_custom_call" | custom-call | flops 268435456 | bytes 7340032 | tf_op jit(solution)/shard_map/pallas_call | solution.py:66
  32.8 0.0 copy-start.7
  32.8 2.8 %collective-permute-start.2 = (bf16[512,256]{1,0:T(8,128)(2,1)S(1)}, bf16[512,256]{1,0:T(8,128)(2,1)S(1)}, u32[]{:S(2)}, u32[]{:S(2)}) collective-permute-start(bf16[512,256]{1,0:T(8,128)(2,1)S(1)} %get-tuple-element.38), channel_id=1, source_target_pairs={{0,128},{1,129},{2,130},{3,131},{4,132},{5,133},{6,134},{7,135},{8... | collective-permute-start | bytes 786440 | tf_op jit(solution)/shard_map/ppermute | solution.py:24
  35.6 3.7 %collective-permute-start.3 = (bf16[512,256]{1,0:T(8,128)(2,1)S(1)}, bf16[512,256]{1,0:T(8,128)(2,1)S(1)}, u32[]{:S(2)}, u32[]{:S(2)}) collective-permute-start(bf16[512,256]{1,0:T(8,128)(2,1)S(1)} %get-tuple-element.39), channel_id=1, source_target_pairs={{0,384},{1,385},{2,386},{3,387},{4,388},{5,389},{6,390},{7,391},{8... | collective-permute-start | bytes 786440 | tf_op jit(solution)/shard_map/ppermute | solution.py:24
  39.3 3.7 %collective-permute-start.4 = (bf16[512,256]{1,0:T(8,128)(2,1)S(1)}, bf16[512,256]{1,0:T(8,128)(2,1)S(1)}, u32[]{:S(2)}, u32[]{:S(2)}) collective-permute-start(bf16[512,256]{1,0:T(8,128)(2,1)S(1)} %get-tuple-element.40), channel_id=1, source_target_pairs={{0,256},{1,257},{2,258},{3,259},{4,260},{5,261},{6,262},{7,263},{8... | collective-permute-start | bytes 786440 | tf_op jit(solution)/shard_map/ppermute | solution.py:24
  43.0 0.0 collective-permute-done.6
  43.0 0.0 collective-permute-done.7
  43.0 0.1 add_convert_fusion
  43.1 5.1 %collective-permute-start.8 = (bf16[256,256]{1,0:T(8,128)(2,1)S(1)}, bf16[256,256]{1,0:T(8,128)(2,1)S(1)}, u32[]{:S(2)}, u32[]{:S(2)}) collective-permute-start(bf16[256,256]{1,0:T(8,128)(2,1)S(1)} %get-tuple-element.45), channel_id=1, source_target_pairs={{0,64},{1,65},{2,66},{3,67},{4,68},{5,69},{6,70},{7,71},{8,72},{9,... | collective-permute-start | bytes 393224 | tf_op jit(solution)/shard_map/ppermute | solution.py:24
  48.2 2.4 %collective-permute-start.9 = (bf16[256,256]{1,0:T(8,128)(2,1)S(1)}, bf16[256,256]{1,0:T(8,128)(2,1)S(1)}, u32[]{:S(2)}, u32[]{:S(2)}) collective-permute-start(bf16[256,256]{1,0:T(8,128)(2,1)S(1)} %get-tuple-element.46), channel_id=1, source_target_pairs={{0,65},{1,66},{2,67},{3,68},{4,69},{5,70},{6,71},{7,72},{8,73},{9,... | collective-permute-start | bytes 393224 | tf_op jit(solution)/shard_map/ppermute | solution.py:24
  50.7 0.0 collective-permute-done.2
  50.7 0.1 add_convert_fusion.2
  50.8 3.2 %collective-permute-start.10 = (bf16[256,256]{1,0:T(8,128)(2,1)S(1)}, bf16[256,256]{1,0:T(8,128)(2,1)S(1)}, u32[]{:S(2)}, u32[]{:S(2)}) collective-permute-start(bf16[256,256]{1,0:T(8,128)(2,1)S(1)} %add_convert_fusion.2), channel_id=1, source_target_pairs={{0,1},{1,2},{2,3},{3,4},{4,5},{5,6},{6,7},{7,8},{8,9},{9,10},{10,1... | collective-permute-start | bytes 393224 | tf_op jit(solution)/shard_map/ppermute | solution.py:24
  54.0 10.7 %collective-permute-done.9 = bf16[256,256]{1,0:T(8,128)(2,1)S(1)} collective-permute-done((bf16[256,256]{1,0:T(8,128)(2,1)S(1)}, bf16[256,256]{1,0:T(8,128)(2,1)S(1)}, u32[]{:S(2)}, u32[]{:S(2)}) %collective-permute-start.9) | collective-permute-done | bytes 131104 | tf_op jit(solution)/shard_map/ppermute | solution.py:24
  64.7 0.9 %fusion.1 = bf16[256,256]{1,0:T(8,128)(2,1)} fusion(bf16[256,256]{1,0:T(8,128)(2,1)S(1)} %copy-done, bf16[256,256]{1,0:T(8,128)(2,1)S(1)} %collective-permute-done.10, bf16[256,256]{1,0:T(8,128)(2,1)S(1)} %collective-permute-done.9, bf16[256,256]{1,0:T(8,128)(2,1)S(1)} %collective-permute-done.8, bf16[512,256]{1,0:T(8,128)(2,1)S(1)} %collective-permute-done.4, ...), kind=kOutput, calls=%fused_computation.2 | convolution fusion | flops 34668544 | bytes 1180672 | tf_op jit(solution)/shard_map/dot_general | solution.py:125
  (20 shorter events, 0.1 us)
Async XLA Ops:
  0.0 64.7 %copy-start = (bf16[256,256]{1,0:T(8,128)(2,1)S(1)}, bf16[256,256]{1,0:T(8,128)(2,1)}, u32[]{:S(2)}) copy-start(bf16[256,256]{1,0:T(8,128)(2,1)} %param.14) | copy-start | bytes 393220
  0.0 14.5 %collective-permute-start.1 = (bf16[64,128,128]{2,1,0:T(8,128)(2,1)}, bf16[64,128,128]{2,1,0:T(8,128)(2,1)S(1)}, u32[]{:S(2)}, u32[]{:S(2)}) collective-permute-start(bf16[64,128,128]{2,1,0:T(8,128)(2,1)} %tiles_a.3), channel_id=1, source_target_pairs={{0,32},{1,33},{2,34},{3,35},{4,36},{5,37},{6,38},{7,39},{8,40},{9,... | collective-permute-start | bytes 6291464 | tf_op jit(solution)/shard_map/ppermute | solution.py:24
  11.3 3.3 %collective-permute-start = (bf16[272,256]{1,0:T(8,128)(2,1)S(1)}, bf16[272,256]{1,0:T(8,128)(2,1)S(1)}, u32[]{:S(2)}, u32[]{:S(2)}) collective-permute-start(bf16[272,256]{1,0:T(8,128)(2,1)S(1)} %pad_maximum_fusion), channel_id=1, source_target_pairs={{0,32},{1,33},{2,34},{3,35},{4,36},{5,37},{6,38},{7,39},{8,40},{9,... | collective-permute-start | bytes 417800 | tf_op jit(solution)/shard_map/ppermute | solution.py:24
  14.6 1.6 %copy-start.1 = (bf16[64,128,128]{2,1,0:T(8,128)(2,1)S(1)}, bf16[64,128,128]{2,1,0:T(8,128)(2,1)}, u32[]{:S(2)}) copy-start(bf16[64,128,128]{2,1,0:T(8,128)(2,1)} %tiles_a.3) | copy-start | bytes 6291460
  16.1 0.9 %copy-start.3 = (bf16[256,256]{1,0:T(8,128)(2,1)S(1)}, bf16[256,256]{1,0:T(8,128)(2,1)}, u32[]{:S(2)}) copy-start(bf16[256,256]{1,0:T(8,128)(2,1)} %param.10) | copy-start | bytes 393220
  17.1 0.7 copy-start.4
  17.7 0.7 copy-start.6
  18.4 11.6 %copy-start.2 = (bf16[64,128,128]{2,1,0:T(8,128)(2,1)S(1)}, bf16[64,128,128]{2,1,0:T(8,128)(2,1)}, u32[]{:S(2)}) copy-start(bf16[64,128,128]{2,1,0:T(8,128)(2,1)} %tiles_a.3) | copy-start | bytes 6291460
  18.4 11.6 %copy-start.5 = (s32[64]{0:T(128)S(1)}, s32[64]{0:T(128)}, u32[]{:S(2)}) copy-start(s32[64]{0:T(128)} %dst_a.3) | copy-start | bytes 772
  21.5 17.8 %collective-permute-start.5 = (bf16[512,256]{1,0:T(8,128)(2,1)S(1)}, bf16[512,256]{1,0:T(8,128)(2,1)S(1)}, u32[]{:S(2)}, u32[]{:S(2)}) collective-permute-start(bf16[512,256]{1,0:T(8,128)(2,1)S(1)} %get-tuple-element.42), channel_id=1, source_target_pairs={{0,128},{1,129},{2,130},{3,131},{4,132},{5,133},{6,134},{7,135},{8... | collective-permute-start | bytes 786440 | tf_op jit(solution)/shard_map/ppermute | solution.py:24
  23.4 19.6 %collective-permute-start.6 = (bf16[512,256]{1,0:T(8,128)(2,1)S(1)}, bf16[512,256]{1,0:T(8,128)(2,1)S(1)}, u32[]{:S(2)}, u32[]{:S(2)}) collective-permute-start(bf16[512,256]{1,0:T(8,128)(2,1)S(1)} %get-tuple-element.43), channel_id=1, source_target_pairs={{0,384},{1,385},{2,386},{3,387},{4,388},{5,389},{6,390},{7,391},{8... | collective-permute-start | bytes 786440 | tf_op jit(solution)/shard_map/ppermute | solution.py:24
  28.0 15.0 %collective-permute-start.7 = (bf16[512,256]{1,0:T(8,128)(2,1)S(1)}, bf16[512,256]{1,0:T(8,128)(2,1)S(1)}, u32[]{:S(2)}, u32[]{:S(2)}) collective-permute-start(bf16[512,256]{1,0:T(8,128)(2,1)S(1)} %get-tuple-element.44), channel_id=1, source_target_pairs={{0,256},{1,257},{2,258},{3,259},{4,260},{5,261},{6,262},{7,263},{8... | collective-permute-start | bytes 786440 | tf_op jit(solution)/shard_map/ppermute | solution.py:24
  32.8 31.9 %copy-start.7 = (f32[256]{0:T(256)S(1)}, f32[256]{0:T(256)}, u32[]{:S(2)}) copy-start(f32[256]{0:T(256)} %param.15) | copy-start | bytes 3076
  32.8 17.9 %collective-permute-start.2 = (bf16[512,256]{1,0:T(8,128)(2,1)S(1)}, bf16[512,256]{1,0:T(8,128)(2,1)S(1)}, u32[]{:S(2)}, u32[]{:S(2)}) collective-permute-start(bf16[512,256]{1,0:T(8,128)(2,1)S(1)} %get-tuple-element.38), channel_id=1, source_target_pairs={{0,128},{1,129},{2,130},{3,131},{4,132},{5,133},{6,134},{7,135},{8... | collective-permute-start | bytes 786440 | tf_op jit(solution)/shard_map/ppermute | solution.py:24
  35.6 15.1 %collective-permute-start.3 = (bf16[512,256]{1,0:T(8,128)(2,1)S(1)}, bf16[512,256]{1,0:T(8,128)(2,1)S(1)}, u32[]{:S(2)}, u32[]{:S(2)}) collective-permute-start(bf16[512,256]{1,0:T(8,128)(2,1)S(1)} %get-tuple-element.39), channel_id=1, source_target_pairs={{0,384},{1,385},{2,386},{3,387},{4,388},{5,389},{6,390},{7,391},{8... | collective-permute-start | bytes 786440 | tf_op jit(solution)/shard_map/ppermute | solution.py:24
  39.3 11.4 %collective-permute-start.4 = (bf16[512,256]{1,0:T(8,128)(2,1)S(1)}, bf16[512,256]{1,0:T(8,128)(2,1)S(1)}, u32[]{:S(2)}, u32[]{:S(2)}) collective-permute-start(bf16[512,256]{1,0:T(8,128)(2,1)S(1)} %get-tuple-element.40), channel_id=1, source_target_pairs={{0,256},{1,257},{2,258},{3,259},{4,260},{5,261},{6,262},{7,263},{8... | collective-permute-start | bytes 786440 | tf_op jit(solution)/shard_map/ppermute | solution.py:24
  43.1 10.8 %collective-permute-start.8 = (bf16[256,256]{1,0:T(8,128)(2,1)S(1)}, bf16[256,256]{1,0:T(8,128)(2,1)S(1)}, u32[]{:S(2)}, u32[]{:S(2)}) collective-permute-start(bf16[256,256]{1,0:T(8,128)(2,1)S(1)} %get-tuple-element.45), channel_id=1, source_target_pairs={{0,64},{1,65},{2,66},{3,67},{4,68},{5,69},{6,70},{7,71},{8,72},{9,... | collective-permute-start | bytes 393224 | tf_op jit(solution)/shard_map/ppermute | solution.py:24
  48.2 16.5 %collective-permute-start.9 = (bf16[256,256]{1,0:T(8,128)(2,1)S(1)}, bf16[256,256]{1,0:T(8,128)(2,1)S(1)}, u32[]{:S(2)}, u32[]{:S(2)}) collective-permute-start(bf16[256,256]{1,0:T(8,128)(2,1)S(1)} %get-tuple-element.46), channel_id=1, source_target_pairs={{0,65},{1,66},{2,67},{3,68},{4,69},{5,70},{6,71},{7,72},{8,73},{9,... | collective-permute-start | bytes 393224 | tf_op jit(solution)/shard_map/ppermute | solution.py:24
  50.8 13.9 %collective-permute-start.10 = (bf16[256,256]{1,0:T(8,128)(2,1)S(1)}, bf16[256,256]{1,0:T(8,128)(2,1)S(1)}, u32[]{:S(2)}, u32[]{:S(2)}) collective-permute-start(bf16[256,256]{1,0:T(8,128)(2,1)S(1)} %add_convert_fusion.2), channel_id=1, source_target_pairs={{0,1},{1,2},{2,3},{3,4},{4,5},{5,6},{6,7},{7,8},{8,9},{9,10},{10,1... | collective-permute-start | bytes 393224 | tf_op jit(solution)/shard_map/ppermute | solution.py:24

commit v2 on v0

v2 whole, which is shorter than its diff:
```python
import jax
import jax.numpy as jnp
from jax import lax
from jax.experimental import pallas as pl
from jax.experimental.pallas import tpu as pltpu
from jax.sharding import PartitionSpec as P

N_X, N_HI, N_CORE, N_ROW = 4, 2, 2, 32
AXES = ("col", "row")
GROUP = 8
LOADS = 4


def route(move):
    pairs = []
    for c in range(N_X * N_HI * N_CORE):
        for r in range(N_ROW):
            x, hi, core, row = move(c // 4, (c // 2) % 2, c % 2, r)
            target = ((x % N_X) * 4 + hi * 2 + core) * N_ROW + row % N_ROW
            pairs.append((c * N_ROW + r, target))
    return pairs


def send(block, move):
    return lax.ppermute(block, AXES, route(move))


def half_sums(wanted, features, tiles, tile_dst, tile_src):
    count, size, _ = tiles.shape
    width = features.shape[-1]
    places = N_HI * N_X * 2 * 2
    load = count // LOADS

    def kernel(meta, dst_in, src_in, tiles_in, feats_in, out, acc, held, feats, dst, src, todo, sems):
        copies = [
            pltpu.make_async_copy(dst_in, dst, sems.at[LOADS]),
            pltpu.make_async_copy(src_in, src, sems.at[LOADS + 1]),
            pltpu.make_async_copy(feats_in, feats, sems.at[LOADS + 2]),
        ]
        loads = [
            pltpu.make_async_copy(tiles_in.at[pl.ds(i * load, load)], held.at[pl.ds(i * load, load)], sems.at[i])
            for i in range(LOADS)
        ]
        for copy in copies + loads:
            copy.start()
        x_here, hi_here, core = meta[0], meta[1], meta[2]
        acc[...] = jnp.zeros_like(acc)
        copies[0].wait()
        copies[1].wait()

        def scan(i, n):
            slot = dst[i]
            near = 1 - (((slot >> 3) & 1) ^ hi_here)
            place = near * 16 + (((slot >> 4) - x_here) & 3) * 4 + (slot & 3)
            todo[n] = i | (src[i] << 8) | (place << 16)
            return n + (((slot >> 2) & 1) == core).astype(jnp.int32)

        ends = []
        n = jnp.int32(0)
        for i in range(LOADS):
            n = lax.fori_loop(i * load, (i + 1) * load, scan, n, unroll=8)
            ends.append(n // GROUP)
        for j in range(GROUP - 1):
            todo[n + j] = places << 16
        ends[-1] = (n + GROUP - 1) // GROUP

        def add(g, carry):
            items = [todo[g * GROUP + j] for j in range(GROUP)]
            prods = [
                jnp.dot(held[e & 255], feats[(e >> 8) & 255], preferred_element_type=jnp.float32) for e in items
            ]
            for e, prod in zip(items, prods):
                acc[e >> 16] += prod
            return carry

        copies[2].wait()
        begin = jnp.int32(0)
        for i in range(LOADS):
            loads[i].wait()
            lax.fori_loop(begin, ends[i], add, 0)
            begin = ends[i]
        out[...] = acc[:places].astype(out.dtype)

    smem = pl.BlockSpec(memory_space=pltpu.SMEM)
    hbm = pl.BlockSpec(memory_space=pltpu.HBM)
    col = lax.axis_index("col")
    meta = jnp.stack([col >> 2, (col >> 1) & 1, wanted(col & 1)]).astype(jnp.int32)
    operands = [tile_dst, tile_src, tiles, features.reshape(-1, size, width)]
    operands = [pltpu.with_memory_space_constraint(operand, pltpu.HBM) for operand in operands]
    return pl.pallas_call(
        kernel,
        out_shape=jax.ShapeDtypeStruct((places, size, width), jnp.bfloat16),
        in_specs=[smem] + [hbm] * 4,
        out_specs=pl.BlockSpec(memory_space=pltpu.VMEM),
        scratch_shapes=[
            pltpu.VMEM((places + 1, size, width), jnp.float32),
            pltpu.VMEM(tiles.shape, tiles.dtype),
            pltpu.VMEM((features.shape[0] // size, size, width), features.dtype),
            pltpu.SMEM((count,), jnp.int32),
            pltpu.SMEM((count,), jnp.int32),
            pltpu.SMEM((count + GROUP,), jnp.int32),
            pltpu.SemaphoreType.DMA((LOADS + 3,)),
        ],
        compiler_params=pltpu.CompilerParams(vmem_limit_bytes=32 * 2**20),
        cost_estimate=pl.CostEstimate(flops=32 * 2 * size * size * width, bytes_accessed=5 * 2**20, transcendentals=0),
    )(meta, *operands)


def total(parts):
    result = parts[0].astype(jnp.float32)
    for part in parts[1:]:
        result = result + part.astype(jnp.float32)
    return result


def shards(features, tiles, tile_dst, tile_src, weight, bias):
    size = tiles.shape[1]
    width = features.shape[1]
    operands = (features, tiles, tile_dst, tile_src)
    theirs = half_sums(lambda core: 1 - core, *operands)
    arrived = send(theirs, lambda x, hi, core, row: (x, hi, 1 - core, row))
    mine = half_sums(lambda core: core, *operands)

    def both(first, n):
        return total([mine[first : first + n], arrived[first : first + n]]).astype(jnp.bfloat16)

    def pieces_of(first):
        return lax.optimization_barrier([both(first + 4 * d, 4) for d in range(N_X)])

    def over_x(pieces, order):
        got = [send(pieces[d], lambda x, hi, core, row, d=d: (x + d, hi, core, row)) for d in order]
        return [pieces[0]] + got

    for_away, for_home = pieces_of(0), pieces_of(16)
    away = total(over_x(for_away, (2, 1, 3))).astype(jnp.bfloat16)
    home = over_x(for_home, (1, 3, 2))
    same_row = send(away[:2], lambda x, hi, core, row: (x, 1 - hi, core, row))
    next_row = send(away[2:], lambda x, hi, core, row: (x, 1 - hi, core, row + 1))
    passed = total([part[2:] for part in home]).astype(jnp.bfloat16)
    passed = send(passed, lambda x, hi, core, row: (x, hi, core, row + 1))
    last = [part[:2] for part in home] + [same_row, next_row, passed]
    aggregate = total(last).reshape(2 * size, width)
    mixed = jnp.dot(aggregate.astype(jnp.bfloat16), weight, preferred_element_type=jnp.float32) + bias
    return jnp.maximum(mixed, 0.0).astype(jnp.bfloat16)


def solution(mesh):
    in_specs = (
        P(("col", "row"), None),
        P(("col", "row"), None, None),
        P(("col", "row")),
        P(("col", "row")),
        P(),
        P(),
    )
    out_specs = P(("col", "row"), None)
    return jax.shard_map(shards, mesh=mesh, in_specs=in_specs, out_specs=out_specs, check_vma=False)
```

time: 180 us -> 58.6 us (0.33)
  the two profiles are of different devices: /device:TPU:1 before, /device:TPU:68 now
where the time goes in v2:
time: 58.6 us; the launch traced here: 58.2 us
  starting transfers between devices  39.2 us (67%)
  waiting for transfers between devices  10.1 us (17%)
  Pallas kernels  6.49 us (11%)
  other arithmetic  1.32 us (2%)
  matrix products  0.85 us (1%)
    ppermute x10, starting transfers between devices, send(): return lax.ppermute(block, AXES, route(move))  39.2 us
    ppermute x10, waiting for transfers between devices, send(): return lax.ppermute(block, AXES, route(move))  10.1 us
    pallas_call x2, Pallas kernels, half_sums(): pl.pallas_call(kernel, out_shape=jax.ShapeDtypeStruct((places, size, widt...  6.49 us
  transfers between devices with their start and end apart: 10, of which 3 were waited for; matrix products, arithmetic and copies ran while one was open for 1% of the time, Pallas kernels for 6%

profile of v2, /device:TPU:68, one launch (start us, length us, event | category | flops | bytes accessed | tf_op | source)
XLA Modules:
  0.0 58.2 jit_solution(2238345834993084577)
XLA Ops:
  0.0 0.0 copy-start
  0.0 0.1 pad_add_fusion.2.meta
  0.1 3.2 %shard_map.65 = bf16[32,128,256]{2,1,0:T(8,128)(2,1)S(1)} custom-call(s32[3]{0:T(128)S(1)} %pad_add_fusion.2.meta, s32[64]{0:T(128)} %dst_in.3, s32[64]{0:T(128)} %src_in.3, bf16[64,128,128]{2,1,0:T(8,128)(2,1)} %tiles_in.3, bf16[2,128,256]{2,1,0:T(8,128)(2,1)} %bitcast.8), custom_call_target="tpu_custom_call" | custom-call | flops 268435456 | bytes 5242880 | tf_op jit(solution)/shard_map/pallas_call | solution.py:90
  3.3 2.0 %collective-permute-start = (bf16[32,128,256]{2,1,0:T(8,128)(2,1)S(1)}, bf16[32,128,256]{2,1,0:T(8,128)(2,1)S(1)}, u32[]{:S(2)}, u32[]{:S(2)}) collective-permute-start(bf16[32,128,256]{2,1,0:T(8,128)(2,1)S(1)} %shard_map.65), channel_id=1, source_target_pairs={{0,32},{1,33},{2,34},{3,35},{4,36},{5,37},{6,38},{7,39},{8,40},{9,... | collective-permute-start | bytes 6291464 | tf_op jit(solution)/shard_map/ppermute | solution.py:25
  5.3 0.1 pad_add_fusion.meta
  5.4 3.3 %shard_map.64 = bf16[32,128,256]{2,1,0:T(8,128)(2,1)S(1)} custom-call(s32[3]{0:T(128)S(1)} %pad_add_fusion.meta, s32[64]{0:T(128)} %dst_in.3, s32[64]{0:T(128)} %src_in.3, bf16[64,128,128]{2,1,0:T(8,128)(2,1)} %tiles_in.3, bf16[2,128,256]{2,1,0:T(8,128)(2,1)} %bitcast.9), custom_call_target="tpu_custom_call" | custom-call | flops 268435456 | bytes 5242880 | tf_op jit(solution)/shard_map/pallas_call | solution.py:90
  8.7 0.6 %collective-permute-done = bf16[32,128,256]{2,1,0:T(8,128)(2,1)S(1)} collective-permute-done((bf16[32,128,256]{2,1,0:T(8,128)(2,1)S(1)}, bf16[32,128,256]{2,1,0:T(8,128)(2,1)S(1)}, u32[]{:S(2)}, u32[]{:S(2)}) %collective-permute-start) | collective-permute-done | bytes 2097184 | tf_op jit(solution)/shard_map/ppermute | solution.py:25
  9.3 0.8 %add_convert_fusion.1 = (bf16[4,128,256]{2,1,0:T(8,128)(2,1)S(1)}, bf16[4,128,256]{2,1,0:T(8,128)(2,1)S(1)}, bf16[4,128,256]{2,1,0:T(8,128)(2,1)S(1)}, bf16[4,12...) fusion(bf16[32,128,256]{2,1,0:T(8,128)(2,1)S(1)} %collective-pe, ...), kind=kLoop, calls=%fused_computation.4 | loop fusion | flops 4194304 | bytes 6291456 | tf_op jit(solution)/shard_map/convert_element_type | solution.py:125
  10.2 0.0 copy-start.1
  10.2 2.5 %collective-permute-start.4 = (bf16[4,128,256]{2,1,0:T(8,128)(2,1)S(1)}, bf16[4,128,256]{2,1,0:T(8,128)(2,1)S(1)}, u32[]{:S(2)}, u32[]{:S(2)}) collective-permute-start(bf16[4,128,256]{2,1,0:T(8,128)(2,1)S(1)} %get-tuple-element.18), channel_id=1, source_target_pairs={{0,256},{1,257},{2,258},{3,259},{4,260},{5,261},{6,262},{7,263},{8... | collective-permute-start | bytes 786440 | tf_op jit(solution)/shard_map/ppermute | solution.py:25
  12.7 4.0 %collective-permute-start.5 = (bf16[4,128,256]{2,1,0:T(8,128)(2,1)S(1)}, bf16[4,128,256]{2,1,0:T(8,128)(2,1)S(1)}, u32[]{:S(2)}, u32[]{:S(2)}) collective-permute-start(bf16[4,128,256]{2,1,0:T(8,128)(2,1)S(1)} %get-tuple-element.19), channel_id=1, source_target_pairs={{0,128},{1,129},{2,130},{3,131},{4,132},{5,133},{6,134},{7,135},{8... | collective-permute-start | bytes 786440 | tf_op jit(solution)/shard_map/ppermute | solution.py:25
  16.7 2.2 %collective-permute-start.6 = (bf16[4,128,256]{2,1,0:T(8,128)(2,1)S(1)}, bf16[4,128,256]{2,1,0:T(8,128)(2,1)S(1)}, u32[]{:S(2)}, u32[]{:S(2)}) collective-permute-start(bf16[4,128,256]{2,1,0:T(8,128)(2,1)S(1)} %get-tuple-element.20), channel_id=1, source_target_pairs={{0,384},{1,385},{2,386},{3,387},{4,388},{5,389},{6,390},{7,391},{8... | collective-permute-start | bytes 786440 | tf_op jit(solution)/shard_map/ppermute | solution.py:25
  18.9 3.6 %collective-permute-start.1 = (bf16[4,128,256]{2,1,0:T(8,128)(2,1)S(1)}, bf16[4,128,256]{2,1,0:T(8,128)(2,1)S(1)}, u32[]{:S(2)}, u32[]{:S(2)}) collective-permute-start(bf16[4,128,256]{2,1,0:T(8,128)(2,1)S(1)} %get-tuple-element.14), channel_id=1, source_target_pairs={{0,128},{1,129},{2,130},{3,131},{4,132},{5,133},{6,134},{7,135},{8... | collective-permute-start | bytes 786440 | tf_op jit(solution)/shard_map/ppermute | solution.py:25
  22.6 2.2 %collective-permute-start.2 = (bf16[4,128,256]{2,1,0:T(8,128)(2,1)S(1)}, bf16[4,128,256]{2,1,0:T(8,128)(2,1)S(1)}, u32[]{:S(2)}, u32[]{:S(2)}) collective-permute-start(bf16[4,128,256]{2,1,0:T(8,128)(2,1)S(1)} %get-tuple-element.15), channel_id=1, source_target_pairs={{0,384},{1,385},{2,386},{3,387},{4,388},{5,389},{6,390},{7,391},{8... | collective-permute-start | bytes 786440 | tf_op jit(solution)/shard_map/ppermute | solution.py:25
  24.8 0.0 collective-permute-done.4
  24.8 6.9 %collective-permute-start.3 = (bf16[4,128,256]{2,1,0:T(8,128)(2,1)S(1)}, bf16[4,128,256]{2,1,0:T(8,128)(2,1)S(1)}, u32[]{:S(2)}, u32[]{:S(2)}) collective-permute-start(bf16[4,128,256]{2,1,0:T(8,128)(2,1)S(1)} %get-tuple-element.16), channel_id=1, source_target_pairs={{0,256},{1,257},{2,258},{3,259},{4,260},{5,261},{6,262},{7,263},{8... | collective-permute-start | bytes 786440 | tf_op jit(solution)/shard_map/ppermute | solution.py:25
  31.7 0.0 collective-permute-done.5
  31.7 0.0 collective-permute-done.6
  31.7 0.1 add_convert_fusion
  31.9 10.0 %collective-permute-start.7 = (bf16[2,128,256]{2,1,0:T(8,128)(2,1)S(1)}, bf16[2,128,256]{2,1,0:T(8,128)(2,1)S(1)}, u32[]{:S(2)}, u32[]{:S(2)}) collective-permute-start(bf16[2,128,256]{2,1,0:T(8,128)(2,1)S(1)} %get-tuple-element.29), channel_id=1, source_target_pairs={{0,64},{1,65},{2,66},{3,67},{4,68},{5,69},{6,70},{7,71},{8,72},{9,... | collective-permute-start | bytes 393224 | tf_op jit(solution)/shard_map/ppermute | solution.py:25
  41.9 2.3 %collective-permute-start.8 = (bf16[2,128,256]{2,1,0:T(8,128)(2,1)S(1)}, bf16[2,128,256]{2,1,0:T(8,128)(2,1)S(1)}, u32[]{:S(2)}, u32[]{:S(2)}) collective-permute-start(bf16[2,128,256]{2,1,0:T(8,128)(2,1)S(1)} %get-tuple-element.30), channel_id=1, source_target_pairs={{0,65},{1,66},{2,67},{3,68},{4,69},{5,70},{6,71},{7,72},{8,73},{9,... | collective-permute-start | bytes 393224 | tf_op jit(solution)/shard_map/ppermute | solution.py:25
  44.2 0.0 collective-permute-done.1
  44.3 0.0 collective-permute-done.2
  44.3 0.0 collective-permute-done.3
  44.3 0.1 add_convert_fusion.10
  44.3 3.4 %collective-permute-start.9 = (bf16[2,128,256]{2,1,0:T(8,128)(2,1)S(1)}, bf16[2,128,256]{2,1,0:T(8,128)(2,1)S(1)}, u32[]{:S(2)}, u32[]{:S(2)}) collective-permute-start(bf16[2,128,256]{2,1,0:T(8,128)(2,1)S(1)} %add_convert_fusion.10), channel_id=1, source_target_pairs={{0,1},{1,2},{2,3},{3,4},{4,5},{5,6},{6,7},{7,8},{8,9},{9,10},{10,1... | collective-permute-start | bytes 393224 | tf_op jit(solution)/shard_map/ppermute | solution.py:25
  47.7 4.7 %collective-permute-done.7 = bf16[2,128,256]{2,1,0:T(8,128)(2,1)S(1)} collective-permute-done((bf16[2,128,256]{2,1,0:T(8,128)(2,1)S(1)}, bf16[2,128,256]{2,1,0:T(8,128)(2,1)S(1)}, u32[]{:S(2)}, u32[]{:S(2)}) %collective-permute-start.7) | collective-permute-done | bytes 131104 | tf_op jit(solution)/shard_map/ppermute | solution.py:25
  52.5 4.7 %collective-permute-done.8 = bf16[2,128,256]{2,1,0:T(8,128)(2,1)S(1)} collective-permute-done((bf16[2,128,256]{2,1,0:T(8,128)(2,1)S(1)}, bf16[2,128,256]{2,1,0:T(8,128)(2,1)S(1)}, u32[]{:S(2)}, u32[]{:S(2)}) %collective-permute-start.8) | collective-permute-done | bytes 131104 | tf_op jit(solution)/shard_map/ppermute | solution.py:25
  57.2 0.0 collective-permute-done.9
  57.2 0.1 add_convert_fusion.9
  57.3 0.0 copy-done
  57.4 0.8 %fusion.1 = bf16[256,256]{1,0:T(8,128)(2,1)} fusion(bf16[256,256]{1,0:T(8,128)(2,1)S(1)} %bitcast.10, bf16[256,256]{1,0:T(8,128)(2,1)S(1)} %copy-done, f32[256]{0:T(256)S(1)} %copy-done.1), kind=kOutput, calls=%fused_computation.2 | convolution fusion | flops 33751040 | bytes 394240 | tf_op jit(solution)/shard_map/dot_general | solution.py:143
  (2 shorter events, 0.0 us)
Async XLA Ops:
  0.0 57.3 %copy-start = (bf16[256,256]{1,0:T(8,128)(2,1)S(1)}, bf16[256,256]{1,0:T(8,128)(2,1)}, u32[]{:S(2)}) copy-start(bf16[256,256]{1,0:T(8,128)(2,1)} %param.10) | copy-start | bytes 393220
  3.3 6.1 %collective-permute-start = (bf16[32,128,256]{2,1,0:T(8,128)(2,1)S(1)}, bf16[32,128,256]{2,1,0:T(8,128)(2,1)S(1)}, u32[]{:S(2)}, u32[]{:S(2)}) collective-permute-start(bf16[32,128,256]{2,1,0:T(8,128)(2,1)S(1)} %shard_map.65), channel_id=1, source_target_pairs={{0,32},{1,33},{2,34},{3,35},{4,36},{5,37},{6,38},{7,39},{8,40},{9,... | collective-permute-start | bytes 6291464 | tf_op jit(solution)/shard_map/ppermute | solution.py:25
  10.2 47.2 %copy-start.1 = (f32[256]{0:T(256)S(1)}, f32[256]{0:T(256)}, u32[]{:S(2)}) copy-start(f32[256]{0:T(256)} %param.11) | copy-start | bytes 3076
  10.2 14.6 %collective-permute-start.4 = (bf16[4,128,256]{2,1,0:T(8,128)(2,1)S(1)}, bf16[4,128,256]{2,1,0:T(8,128)(2,1)S(1)}, u32[]{:S(2)}, u32[]{:S(2)}) collective-permute-start(bf16[4,128,256]{2,1,0:T(8,128)(2,1)S(1)} %get-tuple-element.18), channel_id=1, source_target_pairs={{0,256},{1,257},{2,258},{3,259},{4,260},{5,261},{6,262},{7,263},{8... | collective-permute-start | bytes 786440 | tf_op jit(solution)/shard_map/ppermute | solution.py:25
  12.7 19.0 %collective-permute-start.5 = (bf16[4,128,256]{2,1,0:T(8,128)(2,1)S(1)}, bf16[4,128,256]{2,1,0:T(8,128)(2,1)S(1)}, u32[]{:S(2)}, u32[]{:S(2)}) collective-permute-start(bf16[4,128,256]{2,1,0:T(8,128)(2,1)S(1)} %get-tuple-element.19), channel_id=1, source_target_pairs={{0,128},{1,129},{2,130},{3,131},{4,132},{5,133},{6,134},{7,135},{8... | collective-permute-start | bytes 786440 | tf_op jit(solution)/shard_map/ppermute | solution.py:25
  16.7 15.0 %collective-permute-start.6 = (bf16[4,128,256]{2,1,0:T(8,128)(2,1)S(1)}, bf16[4,128,256]{2,1,0:T(8,128)(2,1)S(1)}, u32[]{:S(2)}, u32[]{:S(2)}) collective-permute-start(bf16[4,128,256]{2,1,0:T(8,128)(2,1)S(1)} %get-tuple-element.20), channel_id=1, source_target_pairs={{0,384},{1,385},{2,386},{3,387},{4,388},{5,389},{6,390},{7,391},{8... | collective-permute-start | bytes 786440 | tf_op jit(solution)/shard_map/ppermute | solution.py:25
  18.9 25.3 %collective-permute-start.1 = (bf16[4,128,256]{2,1,0:T(8,128)(2,1)S(1)}, bf16[4,128,256]{2,1,0:T(8,128)(2,1)S(1)}, u32[]{:S(2)}, u32[]{:S(2)}) collective-permute-start(bf16[4,128,256]{2,1,0:T(8,128)(2,1)S(1)} %get-tuple-element.14), channel_id=1, source_target_pairs={{0,128},{1,129},{2,130},{3,131},{4,132},{5,133},{6,134},{7,135},{8... | collective-permute-start | bytes 786440 | tf_op jit(solution)/shard_map/ppermute | solution.py:25
  22.6 21.7 %collective-permute-start.2 = (bf16[4,128,256]{2,1,0:T(8,128)(2,1)S(1)}, bf16[4,128,256]{2,1,0:T(8,128)(2,1)S(1)}, u32[]{:S(2)}, u32[]{:S(2)}) collective-permute-start(bf16[4,128,256]{2,1,0:T(8,128)(2,1)S(1)} %get-tuple-element.15), channel_id=1, source_target_pairs={{0,384},{1,385},{2,386},{3,387},{4,388},{5,389},{6,390},{7,391},{8... | collective-permute-start | bytes 786440 | tf_op jit(solution)/shard_map/ppermute | solution.py:25
  24.8 19.5 %collective-permute-start.3 = (bf16[4,128,256]{2,1,0:T(8,128)(2,1)S(1)}, bf16[4,128,256]{2,1,0:T(8,128)(2,1)S(1)}, u32[]{:S(2)}, u32[]{:S(2)}) collective-permute-start(bf16[4,128,256]{2,1,0:T(8,128)(2,1)S(1)} %get-tuple-element.16), channel_id=1, source_target_pairs={{0,256},{1,257},{2,258},{3,259},{4,260},{5,261},{6,262},{7,263},{8... | collective-permute-start | bytes 786440 | tf_op jit(solution)/shard_map/ppermute | solution.py:25
  31.9 20.6 %collective-permute-start.7 = (bf16[2,128,256]{2,1,0:T(8,128)(2,1)S(1)}, bf16[2,128,256]{2,1,0:T(8,128)(2,1)S(1)}, u32[]{:S(2)}, u32[]{:S(2)}) collective-permute-start(bf16[2,128,256]{2,1,0:T(8,128)(2,1)S(1)} %get-tuple-element.29), channel_id=1, source_target_pairs={{0,64},{1,65},{2,66},{3,67},{4,68},{5,69},{6,70},{7,71},{8,72},{9,... | collective-permute-start | bytes 393224 | tf_op jit(solution)/shard_map/ppermute | solution.py:25
  41.9 15.3 %collective-permute-start.8 = (bf16[2,128,256]{2,1,0:T(8,128)(2,1)S(1)}, bf16[2,128,256]{2,1,0:T(8,128)(2,1)S(1)}, u32[]{:S(2)}, u32[]{:S(2)}) collective-permute-start(bf16[2,128,256]{2,1,0:T(8,128)(2,1)S(1)} %get-tuple-element.30), channel_id=1, source_target_pairs={{0,65},{1,66},{2,67},{3,68},{4,69},{5,70},{6,71},{7,72},{8,73},{9,... | collective-permute-start | bytes 393224 | tf_op jit(solution)/shard_map/ppermute | solution.py:25
  44.3 12.9 %collective-permute-start.9 = (bf16[2,128,256]{2,1,0:T(8,128)(2,1)S(1)}, bf16[2,128,256]{2,1,0:T(8,128)(2,1)S(1)}, u32[]{:S(2)}, u32[]{:S(2)}) collective-permute-start(bf16[2,128,256]{2,1,0:T(8,128)(2,1)S(1)} %add_convert_fusion.10), channel_id=1, source_target_pairs={{0,1},{1,2},{2,3},{3,4},{4,5},{5,6},{6,7},{7,8},{8,9},{9,10},{10,1... | collective-permute-start | bytes 393224 | tf_op jit(solution)/shard_map/ppermute | solution.py:25

commit v3 on v2

--- a/solution.py
+++ b/solution.py
@@ -51,7 +51,7 @@
         def scan(i, n):
             slot = dst[i]
             near = 1 - (((slot >> 3) & 1) ^ hi_here)
-            place = near * 16 + (((slot >> 4) - x_here) & 3) * 4 + (slot & 3)
+            place = near * 16 + (((slot >> 4) ^ x_here) & 3) * 4 + (slot & 3)
             todo[n] = i | (src[i] << 8) | (place << 16)
             return n + (((slot >> 2) & 1) == core).astype(jnp.int32)
 
@@ -128,12 +128,14 @@
         return lax.optimization_barrier([both(first + 4 * d, 4) for d in range(N_X)])
 
     def over_x(pieces, order):
-        got = [send(pieces[d], lambda x, hi, core, row, d=d: (x + d, hi, core, row)) for d in order]
+        got = [send(pieces[d], lambda x, hi, core, row, d=d: (x ^ d, hi, core, row)) for d in order]
         return [pieces[0]] + got
 
-    for_away, for_home = pieces_of(0), pieces_of(16)
-    away = total(over_x(for_away, (2, 1, 3))).astype(jnp.bfloat16)
-    home = over_x(for_home, (1, 3, 2))
+    for_away = pieces_of(0)
+    for_away, arrived, mine = lax.optimization_barrier((for_away, arrived, mine))
+    for_home = pieces_of(16)
+    away = total(over_x(for_away, (2, 3, 1))).astype(jnp.bfloat16)
+    home = over_x(for_home, (3, 1, 2))
     same_row = send(away[:2], lambda x, hi, core, row: (x, 1 - hi, core, row))
     next_row = send(away[2:], lambda x, hi, core, row: (x, 1 - hi, core, row + 1))
     passed = total([part[2:] for part in home]).astype(jnp.bfloat16)

time: 58.6 us -> 57.8 us (0.986)
  the two profiles are of different devices: /device:TPU:68 before, /device:TPU:64 now
where the time goes in v3:
time: 57.8 us; the launch traced here: 57.4 us
  starting transfers between devices  37.6 us (65%)
  waiting for transfers between devices  10.8 us (19%)
  Pallas kernels  6.79 us (12%)
  other arithmetic  1.13 us (2%)
  matrix products  0.85 us (1%)
    ppermute x10, starting transfers between devices, send(): return lax.ppermute(block, AXES, route(move))  37.6 us
    ppermute x10, waiting for transfers between devices, send(): return lax.ppermute(block, AXES, route(move))  10.8 us
    pallas_call x2, Pallas kernels, half_sums(): pl.pallas_call(kernel, out_shape=jax.ShapeDtypeStruct((places, size, widt...  6.79 us
  transfers between devices with their start and end apart: 10, of which 3 were waited for; matrix products, arithmetic and copies ran while one was open for 1% of the time, Pallas kernels for 6%

profile of v3, /device:TPU:64, one launch (start us, length us, event | category | flops | bytes accessed | tf_op | source)
XLA Modules:
  0.0 57.4 jit_solution(111579086367700110)
XLA Ops:
  0.0 0.1 pad_add_fusion.2.meta
  0.1 3.5 %shard_map.65 = bf16[32,128,256]{2,1,0:T(8,128)(2,1)S(1)} custom-call(s32[3]{0:T(128)S(1)} %pad_add_fusion.2.meta, s32[64]{0:T(128)} %dst_in.3, s32[64]{0:T(128)} %src_in.3, bf16[64,128,128]{2,1,0:T(8,128)(2,1)} %tiles_in.3, bf16[2,128,256]{2,1,0:T(8,128)(2,1)} %bitcast.8), custom_call_target="tpu_custom_call" | custom-call | flops 268435456 | bytes 5242880 | tf_op jit(solution)/shard_map/pallas_call | solution.py:90
  3.6 1.9 %collective-permute-start = (bf16[32,128,256]{2,1,0:T(8,128)(2,1)S(1)}, bf16[32,128,256]{2,1,0:T(8,128)(2,1)S(1)}, u32[]{:S(2)}, u32[]{:S(2)}) collective-permute-start(bf16[32,128,256]{2,1,0:T(8,128)(2,1)S(1)} %shard_map.65), channel_id=1, source_target_pairs={{0,32},{1,33},{2,34},{3,35},{4,36},{5,37},{6,38},{7,39},{8,40},{9,... | collective-permute-start | bytes 6291464 | tf_op jit(solution)/shard_map/ppermute | solution.py:25
  5.5 0.1 pad_add_fusion.meta
  5.6 3.3 %shard_map.64 = bf16[32,128,256]{2,1,0:T(8,128)(2,1)S(1)} custom-call(s32[3]{0:T(128)S(1)} %pad_add_fusion.meta, s32[64]{0:T(128)} %dst_in.3, s32[64]{0:T(128)} %src_in.3, bf16[64,128,128]{2,1,0:T(8,128)(2,1)} %tiles_in.3, bf16[2,128,256]{2,1,0:T(8,128)(2,1)} %bitcast.9), custom_call_target="tpu_custom_call" | custom-call | flops 268435456 | bytes 5242880 | tf_op jit(solution)/shard_map/pallas_call | solution.py:90
  8.9 0.8 %collective-permute-done = bf16[32,128,256]{2,1,0:T(8,128)(2,1)S(1)} collective-permute-done((bf16[32,128,256]{2,1,0:T(8,128)(2,1)S(1)}, bf16[32,128,256]{2,1,0:T(8,128)(2,1)S(1)}, u32[]{:S(2)}, u32[]{:S(2)}) %collective-permute-start) | collective-permute-done | bytes 2097184 | tf_op jit(solution)/shard_map/ppermute | solution.py:25
  9.6 0.3 add_convert_fusion.5
  10.0 4.7 %collective-permute-start.4 = (bf16[4,128,256]{2,1,0:T(8,128)(2,1)S(1)}, bf16[4,128,256]{2,1,0:T(8,128)(2,1)S(1)}, u32[]{:S(2)}, u32[]{:S(2)}) collective-permute-start(bf16[4,128,256]{2,1,0:T(8,128)(2,1)S(1)} %get-tuple-element.30), channel_id=1, source_target_pairs={{0,256},{1,257},{2,258},{3,259},{4,260},{5,261},{6,262},{7,263},{8... | collective-permute-start | bytes 786440 | tf_op jit(solution)/shard_map/ppermute | solution.py:25
  14.7 3.0 %collective-permute-start.5 = (bf16[4,128,256]{2,1,0:T(8,128)(2,1)S(1)}, bf16[4,128,256]{2,1,0:T(8,128)(2,1)S(1)}, u32[]{:S(2)}, u32[]{:S(2)}) collective-permute-start(bf16[4,128,256]{2,1,0:T(8,128)(2,1)S(1)} %get-tuple-element.31), channel_id=1, source_target_pairs={{0,384},{1,385},{2,386},{3,387},{4,388},{5,389},{6,390},{7,391},{8... | collective-permute-start | bytes 786440 | tf_op jit(solution)/shard_map/ppermute | solution.py:25
  17.7 1.9 %collective-permute-start.6 = (bf16[4,128,256]{2,1,0:T(8,128)(2,1)S(1)}, bf16[4,128,256]{2,1,0:T(8,128)(2,1)S(1)}, u32[]{:S(2)}, u32[]{:S(2)}) collective-permute-start(bf16[4,128,256]{2,1,0:T(8,128)(2,1)S(1)} %get-tuple-element.32), channel_id=1, source_target_pairs={{0,128},{1,129},{2,130},{3,131},{4,132},{5,133},{6,134},{7,135},{8... | collective-permute-start | bytes 786440 | tf_op jit(solution)/shard_map/ppermute | solution.py:25
  19.6 0.3 add_convert_fusion.1
  19.9 0.0 copy-start.1
  19.9 4.1 %collective-permute-start.1 = (bf16[4,128,256]{2,1,0:T(8,128)(2,1)S(1)}, bf16[4,128,256]{2,1,0:T(8,128)(2,1)S(1)}, u32[]{:S(2)}, u32[]{:S(2)}) collective-permute-start(bf16[4,128,256]{2,1,0:T(8,128)(2,1)S(1)} %get-tuple-element.26), channel_id=1, source_target_pairs={{0,384},{1,385},{2,386},{3,387},{4,388},{5,389},{6,390},{7,391},{8... | collective-permute-start | bytes 786440 | tf_op jit(solution)/shard_map/ppermute | solution.py:25
  24.0 3.3 %collective-permute-start.2 = (bf16[4,128,256]{2,1,0:T(8,128)(2,1)S(1)}, bf16[4,128,256]{2,1,0:T(8,128)(2,1)S(1)}, u32[]{:S(2)}, u32[]{:S(2)}) collective-permute-start(bf16[4,128,256]{2,1,0:T(8,128)(2,1)S(1)} %get-tuple-element.27), channel_id=1, source_target_pairs={{0,128},{1,129},{2,130},{3,131},{4,132},{5,133},{6,134},{7,135},{8... | collective-permute-start | bytes 786440 | tf_op jit(solution)/shard_map/ppermute | solution.py:25
  27.3 0.0 collective-permute-done.4
  27.4 3.0 %collective-permute-start.3 = (bf16[4,128,256]{2,1,0:T(8,128)(2,1)S(1)}, bf16[4,128,256]{2,1,0:T(8,128)(2,1)S(1)}, u32[]{:S(2)}, u32[]{:S(2)}) collective-permute-start(bf16[4,128,256]{2,1,0:T(8,128)(2,1)S(1)} %get-tuple-element.28), channel_id=1, source_target_pairs={{0,256},{1,257},{2,258},{3,259},{4,260},{5,261},{6,262},{7,263},{8... | collective-permute-start | bytes 786440 | tf_op jit(solution)/shard_map/ppermute | solution.py:25
  30.4 0.0 collective-permute-done.5
  30.4 0.0 collective-permute-done.6
  30.4 0.1 add_convert_fusion
  30.6 10.4 %collective-permute-start.7 = (bf16[2,128,256]{2,1,0:T(8,128)(2,1)S(1)}, bf16[2,128,256]{2,1,0:T(8,128)(2,1)S(1)}, u32[]{:S(2)}, u32[]{:S(2)}) collective-permute-start(bf16[2,128,256]{2,1,0:T(8,128)(2,1)S(1)} %get-tuple-element.41), channel_id=1, source_target_pairs={{0,64},{1,65},{2,66},{3,67},{4,68},{5,69},{6,70},{7,71},{8,72},{9,... | collective-permute-start | bytes 393224 | tf_op jit(solution)/shard_map/ppermute | solution.py:25
  41.0 1.9 %collective-permute-start.8 = (bf16[2,128,256]{2,1,0:T(8,128)(2,1)S(1)}, bf16[2,128,256]{2,1,0:T(8,128)(2,1)S(1)}, u32[]{:S(2)}, u32[]{:S(2)}) collective-permute-start(bf16[2,128,256]{2,1,0:T(8,128)(2,1)S(1)} %get-tuple-element.42), channel_id=1, source_target_pairs={{0,65},{1,66},{2,67},{3,68},{4,69},{5,70},{6,71},{7,72},{8,73},{9,... | collective-permute-start | bytes 393224 | tf_op jit(solution)/shard_map/ppermute | solution.py:25
  42.9 0.0 collective-permute-done.1
  42.9 0.0 collective-permute-done.2
  42.9 0.0 collective-permute-done.3
  43.0 0.1 add_convert_fusion.10
  43.0 3.4 %collective-permute-start.9 = (bf16[2,128,256]{2,1,0:T(8,128)(2,1)S(1)}, bf16[2,128,256]{2,1,0:T(8,128)(2,1)S(1)}, u32[]{:S(2)}, u32[]{:S(2)}) collective-permute-start(bf16[2,128,256]{2,1,0:T(8,128)(2,1)S(1)} %add_convert_fusion.10), channel_id=1, source_target_pairs={{0,1},{1,2},{2,3},{3,4},{4,5},{5,6},{6,7},{7,8},{8,9},{9,10},{10,1... | collective-permute-start | bytes 393224 | tf_op jit(solution)/shard_map/ppermute | solution.py:25
  46.4 4.4 %collective-permute-done.7 = bf16[2,128,256]{2,1,0:T(8,128)(2,1)S(1)} collective-permute-done((bf16[2,128,256]{2,1,0:T(8,128)(2,1)S(1)}, bf16[2,128,256]{2,1,0:T(8,128)(2,1)S(1)}, u32[]{:S(2)}, u32[]{:S(2)}) %collective-permute-start.7) | collective-permute-done | bytes 131104 | tf_op jit(solution)/shard_map/ppermute | solution.py:25
  50.9 5.5 %collective-permute-done.8 = bf16[2,128,256]{2,1,0:T(8,128)(2,1)S(1)} collective-permute-done((bf16[2,128,256]{2,1,0:T(8,128)(2,1)S(1)}, bf16[2,128,256]{2,1,0:T(8,128)(2,1)S(1)}, u32[]{:S(2)}, u32[]{:S(2)}) %collective-permute-start.8) | collective-permute-done | bytes 131104 | tf_op jit(solution)/shard_map/ppermute | solution.py:25
  56.4 0.0 collective-permute-done.9
  56.4 0.1 add_convert_fusion.9
  56.5 0.0 copy-done
  56.6 0.9 %fusion.1 = bf16[256,256]{1,0:T(8,128)(2,1)} fusion(bf16[256,256]{1,0:T(8,128)(2,1)S(1)} %bitcast.10, bf16[256,256]{1,0:T(8,128)(2,1)S(1)} %copy-done, f32[256]{0:T(256)S(1)} %copy-done.1), kind=kOutput, calls=%fused_computation.2 | convolution fusion | flops 33751040 | bytes 394240 | tf_op jit(solution)/shard_map/dot_general | solution.py:145
  (3 shorter events, 0.0 us)
Async XLA Ops:
  0.0 56.5 %copy-start = (bf16[256,256]{1,0:T(8,128)(2,1)S(1)}, bf16[256,256]{1,0:T(8,128)(2,1)}, u32[]{:S(2)}) copy-start(bf16[256,256]{1,0:T(8,128)(2,1)} %param.10) | copy-start | bytes 393220
  3.6 6.1 %collective-permute-start = (bf16[32,128,256]{2,1,0:T(8,128)(2,1)S(1)}, bf16[32,128,256]{2,1,0:T(8,128)(2,1)S(1)}, u32[]{:S(2)}, u32[]{:S(2)}) collective-permute-start(bf16[32,128,256]{2,1,0:T(8,128)(2,1)S(1)} %shard_map.65), channel_id=1, source_target_pairs={{0,32},{1,33},{2,34},{3,35},{4,36},{5,37},{6,38},{7,39},{8,40},{9,... | collective-permute-start | bytes 6291464 | tf_op jit(solution)/shard_map/ppermute | solution.py:25
  10.0 17.4 %collective-permute-start.4 = (bf16[4,128,256]{2,1,0:T(8,128)(2,1)S(1)}, bf16[4,128,256]{2,1,0:T(8,128)(2,1)S(1)}, u32[]{:S(2)}, u32[]{:S(2)}) collective-permute-start(bf16[4,128,256]{2,1,0:T(8,128)(2,1)S(1)} %get-tuple-element.30), channel_id=1, source_target_pairs={{0,256},{1,257},{2,258},{3,259},{4,260},{5,261},{6,262},{7,263},{8... | collective-permute-start | bytes 786440 | tf_op jit(solution)/shard_map/ppermute | solution.py:25
  14.7 15.7 %collective-permute-start.5 = (bf16[4,128,256]{2,1,0:T(8,128)(2,1)S(1)}, bf16[4,128,256]{2,1,0:T(8,128)(2,1)S(1)}, u32[]{:S(2)}, u32[]{:S(2)}) collective-permute-start(bf16[4,128,256]{2,1,0:T(8,128)(2,1)S(1)} %get-tuple-element.31), channel_id=1, source_target_pairs={{0,384},{1,385},{2,386},{3,387},{4,388},{5,389},{6,390},{7,391},{8... | collective-permute-start | bytes 786440 | tf_op jit(solution)/shard_map/ppermute | solution.py:25
  17.7 12.7 %collective-permute-start.6 = (bf16[4,128,256]{2,1,0:T(8,128)(2,1)S(1)}, bf16[4,128,256]{2,1,0:T(8,128)(2,1)S(1)}, u32[]{:S(2)}, u32[]{:S(2)}) collective-permute-start(bf16[4,128,256]{2,1,0:T(8,128)(2,1)S(1)} %get-tuple-element.32), channel_id=1, source_target_pairs={{0,128},{1,129},{2,130},{3,131},{4,132},{5,133},{6,134},{7,135},{8... | collective-permute-start | bytes 786440 | tf_op jit(solution)/shard_map/ppermute | solution.py:25
  19.9 36.6 %copy-start.1 = (f32[256]{0:T(256)S(1)}, f32[256]{0:T(256)}, u32[]{:S(2)}) copy-start(f32[256]{0:T(256)} %param.11) | copy-start | bytes 3076
  19.9 23.0 %collective-permute-start.1 = (bf16[4,128,256]{2,1,0:T(8,128)(2,1)S(1)}, bf16[4,128,256]{2,1,0:T(8,128)(2,1)S(1)}, u32[]{:S(2)}, u32[]{:S(2)}) collective-permute-start(bf16[4,128,256]{2,1,0:T(8,128)(2,1)S(1)} %get-tuple-element.26), channel_id=1, source_target_pairs={{0,384},{1,385},{2,386},{3,387},{4,388},{5,389},{6,390},{7,391},{8... | collective-permute-start | bytes 786440 | tf_op jit(solution)/shard_map/ppermute | solution.py:25
  24.0 18.9 %collective-permute-start.2 = (bf16[4,128,256]{2,1,0:T(8,128)(2,1)S(1)}, bf16[4,128,256]{2,1,0:T(8,128)(2,1)S(1)}, u32[]{:S(2)}, u32[]{:S(2)}) collective-permute-start(bf16[4,128,256]{2,1,0:T(8,128)(2,1)S(1)} %get-tuple-element.27), channel_id=1, source_target_pairs={{0,128},{1,129},{2,130},{3,131},{4,132},{5,133},{6,134},{7,135},{8... | collective-permute-start | bytes 786440 | tf_op jit(solution)/shard_map/ppermute | solution.py:25
  27.4 15.6 %collective-permute-start.3 = (bf16[4,128,256]{2,1,0:T(8,128)(2,1)S(1)}, bf16[4,128,256]{2,1,0:T(8,128)(2,1)S(1)}, u32[]{:S(2)}, u32[]{:S(2)}) collective-permute-start(bf16[4,128,256]{2,1,0:T(8,128)(2,1)S(1)} %get-tuple-element.28), channel_id=1, source_target_pairs={{0,256},{1,257},{2,258},{3,259},{4,260},{5,261},{6,262},{7,263},{8... | collective-permute-start | bytes 786440 | tf_op jit(solution)/shard_map/ppermute | solution.py:25
  30.6 20.3 %collective-permute-start.7 = (bf16[2,128,256]{2,1,0:T(8,128)(2,1)S(1)}, bf16[2,128,256]{2,1,0:T(8,128)(2,1)S(1)}, u32[]{:S(2)}, u32[]{:S(2)}) collective-permute-start(bf16[2,128,256]{2,1,0:T(8,128)(2,1)S(1)} %get-tuple-element.41), channel_id=1, source_target_pairs={{0,64},{1,65},{2,66},{3,67},{4,68},{5,69},{6,70},{7,71},{8,72},{9,... | collective-permute-start | bytes 393224 | tf_op jit(solution)/shard_map/ppermute | solution.py:25
  41.0 15.4 %collective-permute-start.8 = (bf16[2,128,256]{2,1,0:T(8,128)(2,1)S(1)}, bf16[2,128,256]{2,1,0:T(8,128)(2,1)S(1)}, u32[]{:S(2)}, u32[]{:S(2)}) collective-permute-start(bf16[2,128,256]{2,1,0:T(8,128)(2,1)S(1)} %get-tuple-element.42), channel_id=1, source_target_pairs={{0,65},{1,66},{2,67},{3,68},{4,69},{5,70},{6,71},{7,72},{8,73},{9,... | collective-permute-start | bytes 393224 | tf_op jit(solution)/shard_map/ppermute | solution.py:25
  43.0 13.4 %collective-permute-start.9 = (bf16[2,128,256]{2,1,0:T(8,128)(2,1)S(1)}, bf16[2,128,256]{2,1,0:T(8,128)(2,1)S(1)}, u32[]{:S(2)}, u32[]{:S(2)}) collective-permute-start(bf16[2,128,256]{2,1,0:T(8,128)(2,1)S(1)} %add_convert_fusion.10), channel_id=1, source_target_pairs={{0,1},{1,2},{2,3},{3,4},{4,5},{5,6},{6,7},{7,8},{8,9},{9,10},{10,1... | collective-permute-start | bytes 393224 | tf_op jit(solution)/shard_map/ppermute | solution.py:25
